TPU v7x, 32 devices: a whole 2x2x4 slice. The times are simulated.
32 devices in a mesh: lon: 8 (over z, y), lat: 4 (over x, core).
Axes of the slice: x: 2, y: 2, z: 4, core: 2. Of those that a mesh axis runs over, the one named last changes fastest.
Arguments:
- queries: bfloat16 [4, 8, 384, 128], P('lat', 'lon'), may hold values from -4.6 to 4.6
- keys: bfloat16 [4, 8, 384, 128], P('lat', 'lon'), may hold values from -4.6 to 4.6
- values: bfloat16 [4, 8, 384, 128], P('lat', 'lon'), may hold values from -6 to 6
- cotangent: bfloat16 [4, 8, 384, 128], P('lat', 'lon'), may hold values from -384 to 384
- key_tiles: int32 [4, 8, 21], replicated, may hold values from 0 to 31, as said below
- tile_count: int32 [4, 8], replicated, may hold values from 2 to 21, as said below
Outputs:
- grad_queries: bfloat16 [4, 8, 384, 128], P('lat', 'lon')
- grad_keys: bfloat16 [4, 8, 384, 128], P('lat', 'lon')
- grad_values: bfloat16 [4, 8, 384, 128], P('lat', 'lon')
Inputs may be any that keep to these rules, and one draw needn't show every extreme that they name: `key_tiles`: entries are tile ids. The first tile_count entries of tile (a, b) are distinct, include (a, b) itself, and name tiles of bands a - 1 to a + 1 whose longitude lies within 3 tiles of b around the cycle; later entries are tile ids. `tile_count`: some tiles list all 21 entries.
All inputs are finite; a program needn't handle non-finite values.
Results may differ from a plain program's by a relative error of at most 0.0067.
Values may be sent and summed in bfloat16 or wider, within the bound.
A program may use at most 64 MiB of HBM per device.

v0:
```python
import jax
import jax.numpy as jnp
from jax import lax
from jax.sharding import PartitionSpec as P

REACH = 3


NEG_BIG = -1e30


def from_behind(x, axis, by):
    peers = lax.axis_size(axis)
    return lax.ppermute(x, axis, [(i, (i + by) % peers) for i in range(peers)])


def extended(x, sides, width):
    for axis, dim in sides:
        peers, length = (lax.axis_size(axis), x.shape[dim])
        up = [(i, (i + 1) % peers) for i in range(peers - 1)]
        down = [(j, i) for i, j in up]
        last = lax.slice_in_dim(x, length - width, length, axis=dim)
        leading = lax.slice_in_dim(x, 0, width, axis=dim)
        before = lax.ppermute(last, axis, up)
        after = lax.ppermute(leading, axis, down)
        x = jnp.concatenate([before, x, after], axis=dim)
    return x


def passed_along(x, axis, by):
    peers = lax.axis_size(axis)
    pairs = [(i, i + by) for i in range(peers) if 0 <= i + by < peers]
    return lax.ppermute(x, axis, pairs)


def spread_keys(stacked, reach_tiles):
    moving = from_behind(stacked, "lon", reach_tiles)
    blocks = [moving]
    for hop_index in range(2 * reach_tiles):
        moving = from_behind(moving, "lon", -1)
        blocks.append(moving)
    return jnp.stack(blocks)


def gather_home(partial_value, reach_tiles, window_len):
    carried = partial_value[window_len - 1]
    for lon_slot in range(window_len - 2, -1, -1):
        carried = from_behind(carried, "lon", 1) + partial_value[lon_slot]
    arrived = from_behind(carried, "lon", -reach_tiles)
    return arrived


def candidate_tile(windows, candidate, window_len, tile_rows):
    picked = lax.dynamic_index_in_dim(windows, candidate % window_len, 0, keepdims=False)
    return lax.dynamic_slice_in_dim(picked, candidate // window_len * tile_rows, tile_rows, 1)


def pair_terms(query_rows, grad_rows, key_tile, value_tile, norm_rows, delta_vals, score_scale):
    logits = (
        jnp.einsum("qd,kd->qk", query_rows, key_tile, preferred_element_type=jnp.float32)
        * score_scale
    )
    probs = jnp.exp(logits - norm_rows[:, None])
    grad_prob = jnp.einsum("qd,kd->qk", grad_rows, value_tile, preferred_element_type=jnp.float32)
    grad_logit = (probs * (grad_prob - delta_vals[:, None])).astype(jnp.bfloat16)
    return (probs.astype(jnp.bfloat16), grad_logit)


def per_device(queries, keys, values, cotangent, key_tiles, tile_count):
    tile_rows = queries.shape[2]
    head_width = queries.shape[3]
    reach_tiles = REACH
    window_len = 2 * reach_tiles + 1
    lat_tiles = lax.axis_size("lat")
    lon_tiles = lax.axis_size("lon")
    my_band = lax.axis_index("lat")
    my_column = lax.axis_index("lon")
    score_scale = head_width ** (-0.5)
    own_queries = queries.reshape(tile_rows, head_width)
    own_keys = keys.reshape(tile_rows, head_width)
    own_values = values.reshape(tile_rows, head_width)
    own_grads = cotangent.reshape(tile_rows, head_width)
    stacked = jnp.stack([own_keys, own_values])
    banded = extended(stacked, (("lat", 1),), tile_rows)
    windows = spread_keys(banded, reach_tiles)
    tile_table = key_tiles.reshape(lat_tiles * lon_tiles, -1)
    tile_totals = tile_count.reshape(-1)
    slot_count = tile_table.shape[1]
    own_tile = my_band * lon_tiles + my_column
    candidates = jnp.arange(3 * window_len, dtype=jnp.int32)
    cand_band = my_band + candidates // window_len - 1
    cand_column = (my_column + candidates % window_len - reach_tiles) % lon_tiles
    cand_ids = cand_band * lon_tiles + cand_column
    inside = (cand_band >= 0) & (cand_band < lat_tiles)
    slot_live = jnp.arange(slot_count, dtype=jnp.int32)[None, :] < tile_totals[:, None]
    own_list = lax.dynamic_index_in_dim(tile_table, own_tile, 0, keepdims=False)
    own_live = lax.dynamic_index_in_dim(slot_live, own_tile, 0, keepdims=False)
    listed = jnp.any((own_list[None, :] == cand_ids[:, None]) & own_live[None, :], axis=1) & inside

    def first_visit(candidate, running):

        def first_handle(state_now):
            running_max, running_sum, weighted = state_now
            tile_pair = candidate_tile(windows, candidate, window_len, tile_rows)
            logits = (
                jnp.einsum(
                    "qd,kd->qk", own_queries, tile_pair[0], preferred_element_type=jnp.float32
                )
                * score_scale
            )
            grad_prob = jnp.einsum(
                "qd,kd->qk", own_grads, tile_pair[1], preferred_element_type=jnp.float32
            )
            new_max = jnp.maximum(running_max, jnp.max(logits, axis=1))
            rescale = jnp.exp(running_max - new_max)
            powers = jnp.exp(logits - new_max[:, None])
            return (
                new_max,
                running_sum * rescale + jnp.sum(powers, axis=1),
                weighted * rescale + jnp.sum(powers * grad_prob, axis=1),
            )

        return lax.cond(listed[candidate], first_handle, lambda state_now: state_now, running)

    zero_rows = jnp.zeros((tile_rows,), jnp.float32)
    running_max, running_sum, weighted = lax.fori_loop(
        0,
        3 * window_len,
        first_visit,
        (jnp.full((tile_rows,), NEG_BIG, jnp.float32), zero_rows, zero_rows),
    )
    log_norm = running_max + jnp.log(running_sum)
    delta_rows = weighted / running_sum
    zero_index = jnp.zeros((), jnp.int32)
    grad_start = jnp.zeros((tile_rows, head_width), jnp.float32)

    def second_visit(candidate, state_now):

        def second_handle(inner):
            grad_query, partial_value = inner
            tile_pair = candidate_tile(windows, candidate, window_len, tile_rows)
            probs_low, grad_logit = pair_terms(
                own_queries,
                own_grads,
                tile_pair[0],
                tile_pair[1],
                log_norm,
                delta_rows,
                score_scale,
            )
            grad_query = (
                grad_query
                + jnp.einsum(
                    "qk,kd->qd", grad_logit, tile_pair[0], preferred_element_type=jnp.float32
                )
                * score_scale
            )
            key_grad = (
                jnp.einsum("qk,qd->kd", grad_logit, own_queries, preferred_element_type=jnp.float32)
                * score_scale
            )
            value_grad = jnp.einsum(
                "qk,qd->kd", probs_low, own_grads, preferred_element_type=jnp.float32
            )
            fresh_piece = jnp.stack([key_grad, value_grad])[None, None]
            partial_value = lax.dynamic_update_slice(
                partial_value,
                fresh_piece,
                (
                    candidate % window_len,
                    candidate // window_len,
                    zero_index,
                    zero_index,
                    zero_index,
                ),
            )
            return (grad_query, partial_value)

        return lax.cond(listed[candidate], second_handle, lambda inner: inner, state_now)

    partial_start = jnp.zeros((window_len, 3, 2, tile_rows, head_width), jnp.float32)
    grad_query, partial_value = lax.fori_loop(
        0, 3 * window_len, second_visit, (grad_start, partial_start)
    )
    arrived = gather_home(partial_value, reach_tiles, window_len)
    from_lower = passed_along(arrived[2], "lat", 1)
    from_upper = passed_along(arrived[0], "lat", -1)
    key_value = arrived[1] + from_lower + from_upper
    out_shape = (1, 1, tile_rows, head_width)
    return (
        grad_query.astype(jnp.bfloat16).reshape(out_shape),
        key_value[0].astype(jnp.bfloat16).reshape(out_shape),
        key_value[1].astype(jnp.bfloat16).reshape(out_shape),
    )


def solution(mesh):
    in_specs = (
        P("lat", "lon", None, None),
        P("lat", "lon", None, None),
        P("lat", "lon", None, None),
        P("lat", "lon", None, None),
        P(),
        P(),
    )
    out_specs = (
        P("lat", "lon", None, None),
        P("lat", "lon", None, None),
        P("lat", "lon", None, None),
    )
    return jax.shard_map(
        per_device, mesh=mesh, in_specs=in_specs, out_specs=out_specs, check_vma=False
    )
```

profile of v0, /device:TPU:5, one launch (start us, length us, event | category | flops | bytes accessed | tf_op | source)
XLA Modules:
  0.0 535.0 jit_solution(8793095375623690977)
XLA Ops:
  1.6 2.6 collective-permute-start.1
  4.2 3.0 collective-permute-start
  10.8 2.3 collective-permute-start.2
  13.1 13.8 %collective-permute-done.2 = bf16[2,1152,128]{2,1,0:T(8,128)(2,1)S(1)} collective-permute-done((bf16[2,1152,128]{2,1,0:T(8,128)(2,1)S(1)}, bf16[2,1152,128]{2,1,0:T(8,128)(2,1)S(1)}, u32[]{:S(2)}, u32[]{:S(2)}) %collective-permute-start.2) | collective-permute-done | bytes 589856 | tf_op jit(solution)/shard_map/ppermute | solution.py:14
  26.9 11.7 %collective-permute-start.3 = (bf16[2,1152,128]{2,1,0:T(8,128)(2,1)S(1)}, bf16[2,1152,128]{2,1,0:T(8,128)(2,1)S(1)}, u32[]{:S(2)}, u32[]{:S(2)}) collective-permute-start(bf16[2,1152,128]{2,1,0:T(8,128)(2,1)S(1)} %collective-permute-done.2), channel_id=1, source_target_pairs={{0,28},{4,0},{8,4},{12,8},{16,12},{20,16},{24,20},{28,24},{1,29},{... | collective-permute-start | bytes 1769480 | tf_op jit(solution)/shard_map/ppermute | solution.py:14
  38.6 12.8 %collective-permute-done.3 = bf16[2,1152,128]{2,1,0:T(8,128)(2,1)S(1)} collective-permute-done((bf16[2,1152,128]{2,1,0:T(8,128)(2,1)S(1)}, bf16[2,1152,128]{2,1,0:T(8,128)(2,1)S(1)}, u32[]{:S(2)}, u32[]{:S(2)}) %collective-permute-start.3) | collective-permute-done | bytes 589856 | tf_op jit(solution)/shard_map/ppermute | solution.py:14
  51.5 1.9 collective-permute-start.4
  53.4 13.9 %collective-permute-done.4 = bf16[2,1152,128]{2,1,0:T(8,128)(2,1)S(1)} collective-permute-done((bf16[2,1152,128]{2,1,0:T(8,128)(2,1)S(1)}, bf16[2,1152,128]{2,1,0:T(8,128)(2,1)S(1)}, u32[]{:S(2)}, u32[]{:S(2)}) %collective-permute-start.4) | collective-permute-done | bytes 589856 | tf_op jit(solution)/shard_map/ppermute | solution.py:14
  70.2 12.0 %collective-permute-done.5 = bf16[2,1152,128]{2,1,0:T(8,128)(2,1)S(1)} collective-permute-done((bf16[2,1152,128]{2,1,0:T(8,128)(2,1)S(1)}, bf16[2,1152,128]{2,1,0:T(8,128)(2,1)S(1)}, u32[]{:S(2)}, u32[]{:S(2)}) %collective-permute-start.5) | collective-permute-done | bytes 589856 | tf_op jit(solution)/shard_map/ppermute | solution.py:14
  82.7 13.4 %collective-permute-done.6 = bf16[2,1152,128]{2,1,0:T(8,128)(2,1)S(1)} collective-permute-done((bf16[2,1152,128]{2,1,0:T(8,128)(2,1)S(1)}, bf16[2,1152,128]{2,1,0:T(8,128)(2,1)S(1)}, u32[]{:S(2)}, u32[]{:S(2)}) %collective-permute-start.6) | collective-permute-done | bytes 589856 | tf_op jit(solution)/shard_map/ppermute | solution.py:14
  97.2 12.0 %collective-permute-done.7 = bf16[2,1152,128]{2,1,0:T(8,128)(2,1)S(1)} collective-permute-done((bf16[2,1152,128]{2,1,0:T(8,128)(2,1)S(1)}, bf16[2,1152,128]{2,1,0:T(8,128)(2,1)S(1)}, u32[]{:S(2)}, u32[]{:S(2)}) %collective-permute-start.7) | collective-permute-done | bytes 589856 | tf_op jit(solution)/shard_map/ppermute | solution.py:14
  110.7 10.6 %collective-permute-done.8 = bf16[2,1152,128]{2,1,0:T(8,128)(2,1)S(1)} collective-permute-done((bf16[2,1152,128]{2,1,0:T(8,128)(2,1)S(1)}, bf16[2,1152,128]{2,1,0:T(8,128)(2,1)S(1)}, u32[]{:S(2)}, u32[]{:S(2)}) %collective-permute-start.8) | collective-permute-done | bytes 589856 | tf_op jit(solution)/shard_map/ppermute | solution.py:14
  123.3 75.5 %while.32 = (s32[]{:T(128)}, f32[384]{0:T(512)S(1)}, f32[384]{0:T(512)S(1)}, f32[384]{0:T(512)S(1)}, pred[21]{0:T(512)(128)(4,1)S(1)}, /*index=5*/bf16[7,2,1152,...) while((s32[]{:T(128)}, f32[384]{0:T(512)S(1)}, ...), condition=%wide.region_7.8_spmd, body=%wide.region_1.7_spmd.sunk | while | flops 76530832 | bytes 2190819 | solution.py:126
  124.5 2.6 conditional.4
  128.3 2.6 conditional.4
  133.5 2.6 conditional.4
  137.3 2.6 conditional.4
  142.4 2.6 conditional.4
  146.3 2.6 conditional.4
  150.1 2.6 conditional.4
  153.9 2.6 conditional.4
  157.8 2.6 conditional.4
  161.6 2.6 conditional.4
  165.5 2.6 conditional.4
  169.3 2.6 conditional.4
  173.2 2.6 conditional.4
  177.0 2.6 conditional.4
  180.8 2.6 conditional.4
  184.7 2.6 conditional.4
  188.5 2.6 conditional.4
  192.4 2.6 conditional.4
  196.2 2.6 conditional.4
  198.8 4.2 broadcast_in_dim.12
  203.0 119.4 %while.33 = (s32[]{:T(128)}, f32[384,128]{1,0:T(8,128)S(1)}, f32[7,3,2,384,128]{4,3,2,1,0:T(8,128)}, pred[21]{0:T(512)(128)(4,1)S(1)}, bf16[7,2,1152,128]{3,2,1,...) while((s32[]{:T(128)}, f32[384,128]{1,0:T(8,128)S(1)}, ...), condition=%wide.region_11.12_spmd, body=%wide.region_8.11_spmd.sunk | while | flops 189874192 | bytes 4918805 | solution.py:182
  204.3 4.9 conditional.5
  210.4 4.9 conditional.5
  217.8 4.9 conditional.5
  223.9 4.9 conditional.5
  231.4 4.9 conditional.5
  237.5 4.9 conditional.5
  243.6 4.9 conditional.5
  249.8 4.9 conditional.5
  256.0 4.9 conditional.5
  262.1 4.9 conditional.5
  268.3 4.9 conditional.5
  274.4 4.9 conditional.5
  280.6 4.9 conditional.5
  286.7 4.9 conditional.5
  292.9 4.9 conditional.5
  299.0 4.9 conditional.5
  305.1 4.9 conditional.5
  311.3 4.9 conditional.5
  317.4 5.0 conditional.5
  324.0 37.7 %collective-permute-done.9 = f32[3,2,384,128]{3,2,1,0:T(8,128)S(1)} collective-permute-done((f32[3,2,384,128]{3,2,1,0:T(8,128)S(1)}, f32[3,2,384,128]{3,2,1,0:T(8,128)S(1)}, u32[]{:S(2)}, u32[]{:S(2)}) %collective-permute-start.9) | collective-permute-done | bytes 1179680 | tf_op jit(solution)/shard_map/ppermute | solution.py:14
  363.2 25.1 %collective-permute-done.10 = f32[3,2,384,128]{3,2,1,0:T(8,128)S(1)} collective-permute-done((f32[3,2,384,128]{3,2,1,0:T(8,128)S(1)}, f32[3,2,384,128]{3,2,1,0:T(8,128)S(1)}, u32[]{:S(2)}, u32[]{:S(2)}) %collective-permute-start.10) | collective-permute-done | bytes 1179680 | tf_op jit(solution)/shard_map/ppermute | solution.py:14
  389.8 24.9 %collective-permute-done.11 = f32[3,2,384,128]{3,2,1,0:T(8,128)S(1)} collective-permute-done((f32[3,2,384,128]{3,2,1,0:T(8,128)S(1)}, f32[3,2,384,128]{3,2,1,0:T(8,128)S(1)}, u32[]{:S(2)}, u32[]{:S(2)}) %collective-permute-start.11) | collective-permute-done | bytes 1179680 | tf_op jit(solution)/shard_map/ppermute | solution.py:14
  415.0 26.0 %collective-permute-done.12 = f32[3,2,384,128]{3,2,1,0:T(8,128)S(1)} collective-permute-done((f32[3,2,384,128]{3,2,1,0:T(8,128)S(1)}, f32[3,2,384,128]{3,2,1,0:T(8,128)S(1)}, u32[]{:S(2)}, u32[]{:S(2)}) %collective-permute-start.12) | collective-permute-done | bytes 1179680 | tf_op jit(solution)/shard_map/ppermute | solution.py:14
  441.1 33.7 %collective-permute-done.13 = f32[3,2,384,128]{3,2,1,0:T(8,128)S(1)} collective-permute-done((f32[3,2,384,128]{3,2,1,0:T(8,128)S(1)}, f32[3,2,384,128]{3,2,1,0:T(8,128)S(1)}, u32[]{:S(2)}, u32[]{:S(2)}) %collective-permute-start.13) | collective-permute-done | bytes 1179680 | tf_op jit(solution)/shard_map/ppermute | solution.py:14
  475.1 15.0 %collective-permute-done.14 = f32[3,2,384,128]{3,2,1,0:T(8,128)S(1)} collective-permute-done((f32[3,2,384,128]{3,2,1,0:T(8,128)S(1)}, f32[3,2,384,128]{3,2,1,0:T(8,128)S(1)}, u32[]{:S(2)}, u32[]{:S(2)}) %collective-permute-start.14) | collective-permute-done | bytes 1179680 | tf_op jit(solution)/shard_map/ppermute | solution.py:14
  490.3 24.8 %collective-permute-done.15 = f32[3,2,384,128]{3,2,1,0:T(8,128)S(1)} collective-permute-done((f32[3,2,384,128]{3,2,1,0:T(8,128)S(1)}, f32[3,2,384,128]{3,2,1,0:T(8,128)S(1)}, u32[]{:S(2)}, u32[]{:S(2)}) %collective-permute-start.15) | collective-permute-done | bytes 1179680 | tf_op jit(solution)/shard_map/ppermute | solution.py:14
  515.1 10.0 %collective-permute-start.16 = (f32[2,384,128]{2,1,0:T(8,128)S(1)}, f32[2,384,128]{2,1,0:T(8,128)S(1)}, u32[]{:S(2)}, u32[]{:S(2)}) collective-permute-start(f32[2,384,128]{2,1,0:T(8,128)S(1)} %get-tuple-element.412), channel_id=1, source_target_pairs={{0,1},{1,2},{2,3},{4,5},{5,6},{6,7},{8,9},{9,10},{10,11},{12,13},{... | collective-permute-start | bytes 1179656 | tf_op jit(solution)/shard_map/ppermute | solution.py:33
  525.2 1.9 collective-permute-start.17
  527.7 2.1 collective-permute-done.16
  529.9 4.4 collective-permute-done.17
  (329 shorter events, 183.1 us)
Async XLA Ops:
  0.6 68.7 %copy-start = (s32[4,8,21]{2,1,0:T(8,128)S(1)}, s32[4,8,21]{2,1,0:T(8,128)}, u32[]{:S(2)}) copy-start(s32[4,8,21]{2,1,0:T(8,128)} %param.18) | copy-start | bytes 8068
  1.6 7.0 %collective-permute-start.1 = (bf16[2,384,128]{2,1,0:T(8,128)(2,1)S(1)}, bf16[2,384,128]{2,1,0:T(8,128)(2,1)S(1)}, u32[]{:S(2)}, u32[]{:S(2)}) collective-permute-start(bf16[2,384,128]{2,1,0:T(8,128)(2,1)S(1)} %pad_maximum_fusion.1), channel_id=1, source_target_pairs={{1,0},{2,1},{3,2},{5,4},{6,5},{7,6},{9,8},{10,9},{11,10},{13,12},{... | collective-permute-start | bytes 589832 | tf_op jit(solution)/shard_map/ppermute | solution.py:25
  4.2 5.6 %collective-permute-start = (bf16[2,384,128]{2,1,0:T(8,128)(2,1)S(1)}, bf16[2,384,128]{2,1,0:T(8,128)(2,1)S(1)}, u32[]{:S(2)}, u32[]{:S(2)}) collective-permute-start(bf16[2,384,128]{2,1,0:T(8,128)(2,1)S(1)} %pad_maximum_fusion.1), channel_id=1, source_target_pairs={{0,1},{1,2},{2,3},{4,5},{5,6},{6,7},{8,9},{9,10},{10,11},{12,13},{... | collective-permute-start | bytes 589832 | tf_op jit(solution)/shard_map/ppermute | solution.py:24
  10.8 16.1 %collective-permute-start.2 = (bf16[2,1152,128]{2,1,0:T(8,128)(2,1)S(1)}, bf16[2,1152,128]{2,1,0:T(8,128)(2,1)S(1)}, u32[]{:S(2)}, u32[]{:S(2)}) collective-permute-start(bf16[2,1152,128]{2,1,0:T(8,128)(2,1)S(1)} %pad_maximum_fusion), channel_id=1, source_target_pairs={{0,12},{4,16},{8,20},{12,24},{16,28},{20,0},{24,4},{28,8},{1,13},{... | collective-permute-start | bytes 1769480 | tf_op jit(solution)/shard_map/ppermute | solution.py:14
  26.9 24.5 %collective-permute-start.3 = (bf16[2,1152,128]{2,1,0:T(8,128)(2,1)S(1)}, bf16[2,1152,128]{2,1,0:T(8,128)(2,1)S(1)}, u32[]{:S(2)}, u32[]{:S(2)}) collective-permute-start(bf16[2,1152,128]{2,1,0:T(8,128)(2,1)S(1)} %collective-permute-done.2), channel_id=1, source_target_pairs={{0,28},{4,0},{8,4},{12,8},{16,12},{20,16},{24,20},{28,24},{1,29},{... | collective-permute-start | bytes 1769480 | tf_op jit(solution)/shard_map/ppermute | solution.py:14
  51.5 15.8 %collective-permute-start.4 = (bf16[2,1152,128]{2,1,0:T(8,128)(2,1)S(1)}, bf16[2,1152,128]{2,1,0:T(8,128)(2,1)S(1)}, u32[]{:S(2)}, u32[]{:S(2)}) collective-permute-start(bf16[2,1152,128]{2,1,0:T(8,128)(2,1)S(1)} %collective-permute-done.3), channel_id=1, source_target_pairs={{0,28},{4,0},{8,4},{12,8},{16,12},{20,16},{24,20},{28,24},{1,29},{... | collective-permute-start | bytes 1769480 | tf_op jit(solution)/shard_map/ppermute | solution.py:14
  67.3 14.9 %collective-permute-start.5 = (bf16[2,1152,128]{2,1,0:T(8,128)(2,1)S(1)}, bf16[2,1152,128]{2,1,0:T(8,128)(2,1)S(1)}, u32[]{:S(2)}, u32[]{:S(2)}) collective-permute-start(bf16[2,1152,128]{2,1,0:T(8,128)(2,1)S(1)} %collective-permute-done.4), channel_id=1, source_target_pairs={{0,28},{4,0},{8,4},{12,8},{16,12},{20,16},{24,20},{28,24},{1,29},{... | collective-permute-start | bytes 1769480 | tf_op jit(solution)/shard_map/ppermute | solution.py:14
  70.2 53.1 %copy-start.2 = (bf16[1,1,384,128]{3,2,1,0:T(8,128)(2,1)S(1)}, bf16[1,1,384,128]{3,2,1,0:T(8,128)(2,1)}, u32[]{:S(2)}) copy-start(bf16[1,1,384,128]{3,2,1,0:T(8,128)(2,1)} %param.14) | copy-start | bytes 294916
  70.2 53.1 %copy-start.3 = (bf16[1,1,384,128]{3,2,1,0:T(8,128)(2,1)S(1)}, bf16[1,1,384,128]{3,2,1,0:T(8,128)(2,1)}, u32[]{:S(2)}) copy-start(bf16[1,1,384,128]{3,2,1,0:T(8,128)(2,1)} %param.17) | copy-start | bytes 294916
  82.1 14.0 %collective-permute-start.6 = (bf16[2,1152,128]{2,1,0:T(8,128)(2,1)S(1)}, bf16[2,1152,128]{2,1,0:T(8,128)(2,1)S(1)}, u32[]{:S(2)}, u32[]{:S(2)}) collective-permute-start(bf16[2,1152,128]{2,1,0:T(8,128)(2,1)S(1)} %collective-permute-done.5), channel_id=1, source_target_pairs={{0,28},{4,0},{8,4},{12,8},{16,12},{20,16},{24,20},{28,24},{1,29},{... | collective-permute-start | bytes 1769480 | tf_op jit(solution)/shard_map/ppermute | solution.py:14
  96.1 13.0 %collective-permute-start.7 = (bf16[2,1152,128]{2,1,0:T(8,128)(2,1)S(1)}, bf16[2,1152,128]{2,1,0:T(8,128)(2,1)S(1)}, u32[]{:S(2)}, u32[]{:S(2)}) collective-permute-start(bf16[2,1152,128]{2,1,0:T(8,128)(2,1)S(1)} %collective-permute-done.6), channel_id=1, source_target_pairs={{0,28},{4,0},{8,4},{12,8},{16,12},{20,16},{24,20},{28,24},{1,29},{... | collective-permute-start | bytes 1769480 | tf_op jit(solution)/shard_map/ppermute | solution.py:14
  109.1 12.1 %collective-permute-start.8 = (bf16[2,1152,128]{2,1,0:T(8,128)(2,1)S(1)}, bf16[2,1152,128]{2,1,0:T(8,128)(2,1)S(1)}, u32[]{:S(2)}, u32[]{:S(2)}) collective-permute-start(bf16[2,1152,128]{2,1,0:T(8,128)(2,1)S(1)} %collective-permute-done.7), channel_id=1, source_target_pairs={{0,28},{4,0},{8,4},{12,8},{16,12},{20,16},{24,20},{28,24},{1,29},{... | collective-permute-start | bytes 1769480 | tf_op jit(solution)/shard_map/ppermute | solution.py:14
  121.3 1.9 copy-start.4
  322.4 92.3 %copy-start.1 = (f32[7,3,2,384,128]{4,3,2,1,0:T(8,128)S(1)}, f32[7,3,2,384,128]{4,3,2,1,0:T(8,128)}, u32[]{:S(2)}) copy-start(f32[7,3,2,384,128]{4,3,2,1,0:T(8,128)} %get-tuple-element.373) | copy-start | bytes 24772612
  323.9 37.8 %collective-permute-start.9 = (f32[3,2,384,128]{3,2,1,0:T(8,128)S(1)}, f32[3,2,384,128]{3,2,1,0:T(8,128)S(1)}, u32[]{:S(2)}, u32[]{:S(2)}) collective-permute-start(f32[3,2,384,128]{3,2,1,0:T(8,128)S(1)} %slice_bitcast_fusion), channel_id=1, source_target_pairs={{0,4},{4,8},{8,12},{12,16},{16,20},{20,24},{24,28},{28,0},{1,5},{5... | collective-permute-start | bytes 3538952 | tf_op jit(solution)/shard_map/ppermute | solution.py:14
  363.1 25.2 %collective-permute-start.10 = (f32[3,2,384,128]{3,2,1,0:T(8,128)S(1)}, f32[3,2,384,128]{3,2,1,0:T(8,128)S(1)}, u32[]{:S(2)}, u32[]{:S(2)}) collective-permute-start(f32[3,2,384,128]{3,2,1,0:T(8,128)S(1)} %bitcast_add_fusion.5), channel_id=1, source_target_pairs={{0,4},{4,8},{8,12},{12,16},{16,20},{20,24},{24,28},{28,0},{1,5},{5... | collective-permute-start | bytes 3538952 | tf_op jit(solution)/shard_map/ppermute | solution.py:14
  389.8 25.0 %collective-permute-start.11 = (f32[3,2,384,128]{3,2,1,0:T(8,128)S(1)}, f32[3,2,384,128]{3,2,1,0:T(8,128)S(1)}, u32[]{:S(2)}, u32[]{:S(2)}) collective-permute-start(f32[3,2,384,128]{3,2,1,0:T(8,128)S(1)} %bitcast_add_fusion.4), channel_id=1, source_target_pairs={{0,4},{4,8},{8,12},{12,16},{16,20},{20,24},{24,28},{28,0},{1,5},{5... | collective-permute-start | bytes 3538952 | tf_op jit(solution)/shard_map/ppermute | solution.py:14
  414.9 26.1 %collective-permute-start.12 = (f32[3,2,384,128]{3,2,1,0:T(8,128)S(1)}, f32[3,2,384,128]{3,2,1,0:T(8,128)S(1)}, u32[]{:S(2)}, u32[]{:S(2)}) collective-permute-start(f32[3,2,384,128]{3,2,1,0:T(8,128)S(1)} %bitcast_add_fusion.3), channel_id=1, source_target_pairs={{0,4},{4,8},{8,12},{12,16},{16,20},{20,24},{24,28},{28,0},{1,5},{5... | collective-permute-start | bytes 3538952 | tf_op jit(solution)/shard_map/ppermute | solution.py:14
  441.1 33.8 %collective-permute-start.13 = (f32[3,2,384,128]{3,2,1,0:T(8,128)S(1)}, f32[3,2,384,128]{3,2,1,0:T(8,128)S(1)}, u32[]{:S(2)}, u32[]{:S(2)}) collective-permute-start(f32[3,2,384,128]{3,2,1,0:T(8,128)S(1)} %bitcast_add_fusion.2), channel_id=1, source_target_pairs={{0,4},{4,8},{8,12},{12,16},{16,20},{20,24},{24,28},{28,0},{1,5},{5... | collective-permute-start | bytes 3538952 | tf_op jit(solution)/shard_map/ppermute | solution.py:14
  475.0 15.1 %collective-permute-start.14 = (f32[3,2,384,128]{3,2,1,0:T(8,128)S(1)}, f32[3,2,384,128]{3,2,1,0:T(8,128)S(1)}, u32[]{:S(2)}, u32[]{:S(2)}) collective-permute-start(f32[3,2,384,128]{3,2,1,0:T(8,128)S(1)} %bitcast_add_fusion.1), channel_id=1, source_target_pairs={{0,4},{4,8},{8,12},{12,16},{16,20},{20,24},{24,28},{28,0},{1,5},{5... | collective-permute-start | bytes 3538952 | tf_op jit(solution)/shard_map/ppermute | solution.py:14
  490.2 24.9 %collective-permute-start.15 = (f32[3,2,384,128]{3,2,1,0:T(8,128)S(1)}, f32[3,2,384,128]{3,2,1,0:T(8,128)S(1)}, u32[]{:S(2)}, u32[]{:S(2)}) collective-permute-start(f32[3,2,384,128]{3,2,1,0:T(8,128)S(1)} %bitcast_add_fusion), channel_id=1, source_target_pairs={{0,20},{4,24},{8,28},{12,0},{16,4},{20,8},{24,12},{28,16},{1,21},{... | collective-permute-start | bytes 3538952 | tf_op jit(solution)/shard_map/ppermute | solution.py:14
  515.1 14.7 %collective-permute-start.16 = (f32[2,384,128]{2,1,0:T(8,128)S(1)}, f32[2,384,128]{2,1,0:T(8,128)S(1)}, u32[]{:S(2)}, u32[]{:S(2)}) collective-permute-start(f32[2,384,128]{2,1,0:T(8,128)S(1)} %get-tuple-element.412), channel_id=1, source_target_pairs={{0,1},{1,2},{2,3},{4,5},{5,6},{6,7},{8,9},{9,10},{10,11},{12,13},{... | collective-permute-start | bytes 1179656 | tf_op jit(solution)/shard_map/ppermute | solution.py:33
  525.2 9.1 %collective-permute-start.17 = (f32[2,384,128]{2,1,0:T(8,128)S(1)}, f32[2,384,128]{2,1,0:T(8,128)S(1)}, u32[]{:S(2)}, u32[]{:S(2)}) collective-permute-start(f32[2,384,128]{2,1,0:T(8,128)S(1)} %get-tuple-element.413), channel_id=1, source_target_pairs={{1,0},{2,1},{3,2},{5,4},{6,5},{7,6},{9,8},{10,9},{11,10},{13,12},{... | collective-permute-start | bytes 1179656 | tf_op jit(solution)/shard_map/ppermute | solution.py:33
where the time goes:
time: 539 us; the launch traced here: 535 us
  waiting for transfers between devices  285 us (53%)
  matrix products  121 us (22%)
  starting transfers between devices  37.2 us (7%)
  local copies, waits for them, and re-layouts  35.1 us (7%)
  loops' own time  31.2 us (6%)
  other arithmetic  24.7 us (5%)
    ppermute x14, waiting for transfers between devices, from_behind(): return lax.ppermute(x, axis, [(i, (i + by) % peers) for i in range(peers)])  276 us
    dot_general x19, matrix products, second_handle(): jnp.einsum('qk,kd->qd', grad_logit, tile_pair[0], preferred_element_type=...  22.7 us
    dot_general x19, matrix products, first_handle(): jnp.einsum('qd,kd->qk', own_grads, tile_pair[1], preferred_element_type=j...  22.5 us
    dot_general x19, matrix products, first_handle(): jnp.einsum('qd,kd->qk', own_queries, tile_pair[0], preferred_element_type...  22.4 us
    dot_general x19, matrix products, pair_terms(): jnp.einsum('qd,kd->qk', query_rows, key_tile, preferred_element_type=jnp....  22.3 us
    dot_general x19, matrix products, pair_terms(): jnp.einsum('qd,kd->qk', grad_rows, value_tile, preferred_element_type=jnp...  22.2 us
    ppermute x14, starting transfers between devices, from_behind(): return lax.ppermute(x, axis, [(i, (i + by) % peers) for i in range(peers)])  19.6 us
    dynamic_update_slice x19, other arithmetic, second_handle(): lax.dynamic_update_slice(partial_value, fresh_piece, (candidate % window_...  15.1 us
  transfers between devices with their start and end apart: 18, of which 18 were waited for; matrix products, arithmetic and copies ran while one was open for 1% of the time, Pallas kernels for 0%

commit v1 on v0

v1 whole, which is shorter than its diff:
```python
import functools

import jax
import jax.numpy as jnp
from jax import lax
from jax.experimental import pallas as pl
from jax.experimental.pallas import tpu as pltpu
from jax.sharding import PartitionSpec as P

MESH = pl.DeviceIdType.MESH
PAIR_STEPS = (0, 1, -1, 2)
BANDS = (0, -1, 1)
BAND_BACK = (0, 2, 1)
UNLISTED = -1e30
LOWEST = -1e20
LOG2E = 1.4426950408889634


def dot_rows(a, b):
    return lax.dot_general(a, b, (((1,), (1,)), ((), ())), preferred_element_type=jnp.float32)


def dot(a, b):
    return jnp.dot(a, b, preferred_element_type=jnp.float32)


def kernel(
    pairs, bands,
    q_ref, k_ref, v_ref, g_ref, list_ref, count_ref,
    dq_ref, dk_ref, dv_ref,
    qbuf, gbuf, kbuf, vbuf, kturn, pstore, gpstore, maxrow, bias, stats, stats_in,
    plow, dslow, dqacc, dkacc, dvacc, dqout, dqin, dkout, dvout, dkin, dvin,
    q_send, q_recv, g_send, g_recv, k_send, k_recv, v_send, v_recv, s_send, s_recv,
    dq_send, dq_recv, dk_send, dk_recv, dv_send, dv_recv,
):
    rows, width = q_ref.shape[2], q_ref.shape[3]
    scale = width ** -0.5
    scale2 = scale * LOG2E
    lon = lax.axis_index("lon")
    lat = lax.axis_index("lat")
    g = lon // 2
    p = lon % 2
    sign = 1 - 2 * p
    ring = 2 * pairs

    def along(step):
        return lax.rem(lon + 2 * sign * step + 2 * ring, ring)

    def column(e):
        return 2 * g + p + e * sign

    def has_band(place):
        below = jnp.where(place == 1, lat > 0, True)
        above = jnp.where(place == 2, lat < bands - 1, True)
        return jnp.logical_and(below, above)

    distances = sorted({e % pairs for e in range(-3, 4)} - {0})

    barrier = pltpu.get_barrier_semaphore()
    for e in distances:
        pl.semaphore_signal(barrier, inc=1, device_id={"lon": along(e), "lat": lat}, device_id_type=MESH)
    beside = [(e, place) for e in (0, 1) for place in range(3) if (e, place) != (0, 0)]
    for e, place in beside:
        @pl.when(has_band(place))
        def _(e=e, place=place):
            pl.semaphore_signal(
                barrier, inc=1,
                device_id={"lon": column(e), "lat": lat + BANDS[place]}, device_id_type=MESH,
            )

    qbuf[0] = q_ref[0, 0]
    gbuf[0] = g_ref[0, 0]
    kbuf[0] = k_ref[0, 0]
    vbuf[0] = v_ref[0, 0]

    slot = lax.broadcasted_iota(jnp.int32, (8, 1), 0)
    other = jnp.where(slot >= 3, 1, 0)
    place = slot - 3 * other
    band = lat + jnp.where(place == 0, 0, jnp.where(place == 1, -1, 1))
    key_ids = band * ring + 2 * g + p + other * sign
    entry = lax.broadcasted_iota(jnp.int32, (1, list_ref.shape[2]), 1)
    lane = lax.broadcasted_iota(jnp.int32, (1, ring), 1)
    counts = count_ref[pl.ds(lat, 1), :]
    for t, step in enumerate(PAIR_STEPS):
        where_q = along(step)
        count = jnp.sum(jnp.where(lane == where_q, counts, 0), axis=1, keepdims=True)
        mine = list_ref[lat, pl.ds(where_q, 1), :]
        hit = jnp.where((mine == key_ids) & (entry < count), 1.0, 0.0)
        found = jnp.max(hit, axis=1, keepdims=True)
        bias[t] = jnp.broadcast_to(jnp.where(found > 0.5, 0.0, UNLISTED), (8, rows))

    stats[0:4] = jnp.full((4, rows), LOWEST, jnp.float32)
    stats[4:16] = jnp.zeros((12, rows), jnp.float32)

    n_beside = 1 + 2 * (jnp.where(lat > 0, 1, 0) + jnp.where(lat < bands - 1, 1, 0))
    pl.semaphore_wait(barrier, len(distances) + n_beside)

    def remote(src, dst, send, recv, to_lon, to_lat):
        return pltpu.make_async_remote_copy(
            src_ref=src, dst_ref=dst, send_sem=send, recv_sem=recv,
            device_id={"lon": to_lon, "lat": to_lat}, device_id_type=MESH,
        )

    def key_copies(e, place):
        here, there = 3 * e + place, 3 * e + BAND_BACK[place]
        to = (column(e), lat + BANDS[place])
        return (
            remote(k_ref.at[0, 0], kbuf.at[there], k_send.at[here], k_recv.at[there], *to),
            remote(v_ref.at[0, 0], vbuf.at[there], v_send.at[here], v_recv.at[there], *to),
        )

    def query_copies(t):
        to = (along(-PAIR_STEPS[t]), lat)
        return (
            remote(q_ref.at[0, 0], qbuf.at[t], q_send.at[t], q_recv.at[t], *to),
            remote(g_ref.at[0, 0], gbuf.at[t], g_send.at[t], g_recv.at[t], *to),
        )

    for t in (1, 2, 3):
        for copy in query_copies(t):
            copy.start()
    for e, place in beside:
        @pl.when(has_band(place))
        def _(e=e, place=place):
            for copy in key_copies(e, place):
                copy.start()

    dqacc[...] = jnp.zeros_like(dqacc)
    dkacc[...] = jnp.zeros_like(dkacc)
    dvacc[...] = jnp.zeros_like(dvacc)

    def arrived(buf, index, recv):
        pltpu.make_async_copy(buf.at[index], buf.at[index], recv.at[index]).wait()

    chunks = [pl.ds(i, 128) for i in range(0, rows, 128)]

    def first_slot(t):
        return 3 if t == 3 else 0

    def stored(t, ks):
        return t * 6 + ks - first_slot(t)

    def first_pair(t, ks):
        index = stored(t, ks)
        logits = dot_rows(kbuf[ks], qbuf[t])
        pstore[index] = logits
        offset = bias[t, pl.ds(ks, 1), :]
        top = jnp.max(logits, axis=0, keepdims=True) * scale2 + offset
        old = stats[t:t + 1]
        new = jnp.maximum(old, top)
        shift = new - offset
        gpstore[index] = dot_rows(vbuf[ks], gbuf[t])
        total = jnp.zeros((1, rows), jnp.float32)
        weighted = jnp.zeros((1, rows), jnp.float32)
        for c in chunks:
            powers = jnp.exp2(pstore[index, c, :] * scale2 - shift)
            pstore[index, c, :] = powers
            total += jnp.sum(powers, axis=0, keepdims=True)
            weighted += jnp.sum(powers * gpstore[index, c, :], axis=0, keepdims=True)
        shrink = jnp.exp2(old - new)
        maxrow[pl.ds(index, 1), :] = new
        stats[t:t + 1] = new
        stats[4 + t:5 + t] = stats[4 + t:5 + t] * shrink + total
        stats[8 + t:9 + t] = stats[8 + t:9 + t] * shrink + weighted

    for t in range(4):
        if t > 0:
            arrived(qbuf, t, q_recv)
            arrived(gbuf, t, g_recv)

        def first_step(ks, carry, t=t):
            @pl.when(has_band(ks % 3))
            def _():
                if t == 0:
                    @pl.when(ks > 0)
                    def _():
                        arrived(kbuf, ks, k_recv)
                        arrived(vbuf, ks, v_recv)
                    kturn[ks] = kbuf[ks].astype(jnp.float32).T.astype(jnp.bfloat16)
                first_pair(t, ks)
            return carry

        lax.fori_loop(first_slot(t), 6, first_step, 0)

    def stat_copy(i, e):
        back = distances.index(-e % pairs)
        return remote(stats, stats_in.at[back], s_send.at[i], s_recv.at[back], along(e), lat)

    for i, e in enumerate(distances):
        stat_copy(i, e).start()
    for i, e in enumerate(distances):
        arrived(stats_in, i, s_recv)

    finals = []
    for t, step in enumerate(PAIR_STEPS):
        parts = [(stats[t:t + 1], stats[4 + t:5 + t], stats[8 + t:9 + t])]
        for i, e in enumerate(distances):
            for other_t, other_step in enumerate(PAIR_STEPS):
                if (other_step + e - step) % pairs == 0:
                    parts.append(tuple(
                        stats_in[i, r + other_t:r + other_t + 1, :] for r in (0, 4, 8)
                    ))
        top = functools.reduce(jnp.maximum, [m for m, _, _ in parts])
        total = sum(l * jnp.exp2(m - top) for m, l, _ in parts)
        weighted = sum(w * jnp.exp2(m - top) for m, _, w in parts)
        inverse = 1.0 / total
        finals.append((top, inverse, weighted * inverse))

    def second_pair(t, ks):
        index = stored(t, ks)
        top, inverse, delta = finals[t]
        factor = jnp.exp2(maxrow[pl.ds(index, 1), :] - top) * inverse
        for c in chunks:
            probs = pstore[index, c, :] * factor
            plow[c, :] = probs.astype(jnp.bfloat16)
            dslow[c, :] = (probs * (gpstore[index, c, :] - delta)).astype(jnp.bfloat16)
        dvacc[ks] += dot(plow[...], gbuf[t])
        dkacc[ks] += dot(dslow[...], qbuf[t])
        dqacc[t] += dot(kturn[ks], dslow[...])

    def query_grad_copy(t):
        return remote(
            dqout.at[t], dqin.at[t], dq_send.at[t], dq_recv.at[t], along(PAIR_STEPS[t]), lat
        )

    for t in (3, 1, 2):
        def second_step(ks, carry, t=t):
            @pl.when(has_band(ks % 3))
            def _():
                second_pair(t, ks)
            return carry

        lax.fori_loop(first_slot(t), 6, second_step, 0)
        dqout[t] = (dqacc[t] * scale).astype(jnp.bfloat16)
        query_grad_copy(t).start()

    def key_grad_copies(ks):
        e, place = ks // 3, ks % 3
        back = 3 * e + jnp.where(place == 0, 0, 3 - place)
        to = (column(e), lat + jnp.where(place == 0, 0, 2 * place - 3))
        return (
            remote(dkout.at[ks], dkin.at[back], dk_send.at[ks], dk_recv.at[back], *to),
            remote(dvout.at[ks], dvin.at[back], dv_send.at[ks], dv_recv.at[back], *to),
        )

    def last_step(i, carry):
        ks = 5 - i

        @pl.when(has_band(ks % 3))
        def _():
            second_pair(0, ks)

            @pl.when(ks > 0)
            def _():
                dkout[ks] = (dkacc[ks] * scale).astype(jnp.bfloat16)
                dvout[ks] = dvacc[ks].astype(jnp.bfloat16)
                for copy in key_grad_copies(ks):
                    copy.start()
        return carry

    lax.fori_loop(0, 6, last_step, 0)

    total = dqacc[0] * scale
    for t in (3, 1, 2):
        arrived(dqin, t, dq_recv)
        total += dqin[t].astype(jnp.float32)
    dq_ref[0, 0] = total.T.astype(jnp.bfloat16)

    dkacc[0] = dkacc[0] * scale
    for e, place in reversed(beside):
        @pl.when(has_band(place))
        def _(e=e, place=place):
            ks = 3 * e + place
            arrived(dkin, ks, dk_recv)
            arrived(dvin, ks, dv_recv)
            dkacc[0] += dkin[ks].astype(jnp.float32)
            dvacc[0] += dvin[ks].astype(jnp.float32)
    dk_ref[0, 0] = dkacc[0].astype(jnp.bfloat16)
    dv_ref[0, 0] = dvacc[0].astype(jnp.bfloat16)

    for t in (1, 2, 3):
        for copy in query_copies(t):
            copy.wait_send()
        query_grad_copy(t).wait_send()
    for i, e in enumerate(distances):
        stat_copy(i, e).wait_send()
    for e, place in beside:
        @pl.when(has_band(place))
        def _(e=e, place=place):
            for copy in key_copies(e, place) + key_grad_copies(3 * e + place):
                copy.wait_send()


def per_device(pairs, bands, queries, keys, values, cotangent, key_tiles, tile_count):
    rows, width = queries.shape[2], queries.shape[3]
    shape = jax.ShapeDtypeStruct(queries.shape, jnp.bfloat16)
    low, full = jnp.bfloat16, jnp.float32
    n_stats = len({e % pairs for e in range(-3, 4)} - {0})
    vmem = pl.BlockSpec(memory_space=pltpu.VMEM)
    dma = pltpu.SemaphoreType.DMA
    return pl.pallas_call(
        functools.partial(kernel, pairs, bands),
        out_shape=(shape, shape, shape),
        in_specs=[vmem] * 6,
        out_specs=(vmem, vmem, vmem),
        scratch_shapes=[
            pltpu.VMEM((4, rows, width), low),
            pltpu.VMEM((4, rows, width), low),
            pltpu.VMEM((6, rows, width), low),
            pltpu.VMEM((6, rows, width), low),
            pltpu.VMEM((6, width, rows), low),
            pltpu.VMEM((21, rows, rows), full),
            pltpu.VMEM((21, rows, rows), full),
            pltpu.VMEM((24, rows), full),
            pltpu.VMEM((4, 8, rows), full),
            pltpu.VMEM((16, rows), full),
            pltpu.VMEM((n_stats, 16, rows), full),
            pltpu.VMEM((rows, rows), low),
            pltpu.VMEM((rows, rows), low),
            pltpu.VMEM((4, width, rows), full),
            pltpu.VMEM((6, rows, width), full),
            pltpu.VMEM((6, rows, width), full),
            pltpu.VMEM((4, width, rows), low),
            pltpu.VMEM((4, width, rows), low),
            pltpu.VMEM((6, rows, width), low),
            pltpu.VMEM((6, rows, width), low),
            pltpu.VMEM((6, rows, width), low),
            pltpu.VMEM((6, rows, width), low),
            dma((4,)), dma((4,)), dma((4,)), dma((4,)),
            dma((6,)), dma((6,)), dma((6,)), dma((6,)),
            dma((n_stats,)), dma((n_stats,)),
            dma((4,)), dma((4,)),
            dma((6,)), dma((6,)), dma((6,)), dma((6,)),
        ],
        compiler_params=pltpu.CompilerParams(
            collective_id=0, has_side_effects=True, vmem_limit_bytes=48 * 1024 * 1024
        ),
    )(queries, keys, values, cotangent, key_tiles, tile_count)


def solution(mesh):
    tiles = P("lat", "lon", None, None)
    return jax.shard_map(
        functools.partial(per_device, mesh.shape["lon"] // 2, mesh.shape["lat"]),
        mesh=mesh,
        in_specs=(tiles, tiles, tiles, tiles, P(), P()),
        out_specs=(tiles, tiles, tiles),
        check_vma=False,
    )
```

time: 539 us -> 55.3 us (0.10)
  the two profiles are of different devices: /device:TPU:5 before, /device:TPU:1 now
where the time goes in v1:
time: 55.3 us; the launch traced here: 55 us
  Pallas kernels  47.5 us (86%)
  local copies, waits for them, and re-layouts  6.88 us (12%)
  between operations  0.65 us (1%)
    pallas_call x1, Pallas kernels, per_device(): pl.pallas_call(functools.partial(kernel, pairs, bands), out_shape=(shape,...  47.5 us
    unnamed x15, local copies, waits for them, and re-layouts  6.88 us

profile of v1, /device:TPU:1, one launch (start us, length us, event | category | flops | bytes accessed | tf_op | source)
XLA Modules:
  0.0 55.0 jit_solution(3490167443661379920)
XLA Ops:
  0.6 0.0 copy-start
  0.6 0.9 %copy-done = bf16[1,1,384,128]{3,2,1,0:T(8,128)(2,1)S(1)} copy-done((bf16[1,1,384,128]{3,2,1,0:T(8,128)(2,1)S(1)}, bf16[1,1,384,128]{3,2,1,0:T(8,128)(2,1)}, u32[]{:S(2)}) %copy-start) | copy-done | bytes 98328
  1.5 0.0 copy-start.1
  1.5 0.9 %copy-done.1 = bf16[1,1,384,128]{3,2,1,0:T(8,128)(2,1)S(1)} copy-done((bf16[1,1,384,128]{3,2,1,0:T(8,128)(2,1)S(1)}, bf16[1,1,384,128]{3,2,1,0:T(8,128)(2,1)}, u32[]{:S(2)}) %copy-start.1) | copy-done | bytes 98328
  2.4 0.0 copy-start.2
  2.4 0.9 %copy-done.2 = bf16[1,1,384,128]{3,2,1,0:T(8,128)(2,1)S(1)} copy-done((bf16[1,1,384,128]{3,2,1,0:T(8,128)(2,1)S(1)}, bf16[1,1,384,128]{3,2,1,0:T(8,128)(2,1)}, u32[]{:S(2)}) %copy-start.2) | copy-done | bytes 98328
  3.3 0.0 copy-start.3
  3.3 0.9 %copy-done.3 = bf16[1,1,384,128]{3,2,1,0:T(8,128)(2,1)S(1)} copy-done((bf16[1,1,384,128]{3,2,1,0:T(8,128)(2,1)S(1)}, bf16[1,1,384,128]{3,2,1,0:T(8,128)(2,1)}, u32[]{:S(2)}) %copy-start.3) | copy-done | bytes 98328
  4.2 0.0 copy-start.4
  4.2 0.7 %copy-done.4 = s32[4,8,21]{2,1,0:T(8,128)S(1)} copy-done((s32[4,8,21]{2,1,0:T(8,128)S(1)}, s32[4,8,21]{2,1,0:T(8,128)}, u32[]{:S(2)}) %copy-start.4) | copy-done | bytes 2712
  4.9 0.0 copy-start.5
  4.9 0.7 %copy-done.5 = s32[4,8]{1,0:T(4,128)S(1)} copy-done((s32[4,8]{1,0:T(4,128)S(1)}, s32[4,8]{1,0:T(4,128)}, u32[]{:S(2)}) %copy-start.5) | copy-done | bytes 152
  5.6 47.5 %shard_map.85 = (bf16[1,1,384,128]{3,2,1,0:T(8,128)(2,1)S(1)}, bf16[1,1,384,128]{3,2,1,0:T(8,128)(2,1)S(1)}, bf16[1,1,384,128]{3,2,1,0:T(8,128)(2,1)S(1)}) custom-call(bf16[1,1,384,128]{3,2,1,0:T(8,128)(2,1)S(1)} %copy-done, bf16[1,1,384,128]{3,2,1,0:T(8,128)(2,1)S(1)} %copy-done.1, bf16[1,1,384,128]{3,2,1,0:T(8,128)(2,1)S(1)} %copy-done.2, ...), custom_call_target="tpu_custom_call" | custom-call | tf_op jit(solution)/shard_map/pallas_call | solution.py:301
  53.1 0.6 %copy.12 = bf16[1,1,384,128]{3,2,1,0:T(8,128)(2,1)} copy(bf16[1,1,384,128]{3,2,1,0:T(8,128)(2,1)S(1)} %get-tuple-element.6) | data formatting | bytes 196608
  53.7 0.6 %copy.13 = bf16[1,1,384,128]{3,2,1,0:T(8,128)(2,1)} copy(bf16[1,1,384,128]{3,2,1,0:T(8,128)(2,1)S(1)} %get-tuple-element.7) | data formatting | bytes 196608
  54.4 0.6 %copy.14 = bf16[1,1,384,128]{3,2,1,0:T(8,128)(2,1)} copy(bf16[1,1,384,128]{3,2,1,0:T(8,128)(2,1)S(1)} %get-tuple-element.8) | data formatting | bytes 196608
Async XLA Ops:
  0.6 0.9 %copy-start = (bf16[1,1,384,128]{3,2,1,0:T(8,128)(2,1)S(1)}, bf16[1,1,384,128]{3,2,1,0:T(8,128)(2,1)}, u32[]{:S(2)}) copy-start(bf16[1,1,384,128]{3,2,1,0:T(8,128)(2,1)} %q_ref.1) | copy-start | bytes 294916
  1.5 0.9 %copy-start.1 = (bf16[1,1,384,128]{3,2,1,0:T(8,128)(2,1)S(1)}, bf16[1,1,384,128]{3,2,1,0:T(8,128)(2,1)}, u32[]{:S(2)}) copy-start(bf16[1,1,384,128]{3,2,1,0:T(8,128)(2,1)} %k_ref.1) | copy-start | bytes 294916
  2.4 0.9 %copy-start.2 = (bf16[1,1,384,128]{3,2,1,0:T(8,128)(2,1)S(1)}, bf16[1,1,384,128]{3,2,1,0:T(8,128)(2,1)}, u32[]{:S(2)}) copy-start(bf16[1,1,384,128]{3,2,1,0:T(8,128)(2,1)} %v_ref.1) | copy-start | bytes 294916
  3.3 0.9 %copy-start.3 = (bf16[1,1,384,128]{3,2,1,0:T(8,128)(2,1)S(1)}, bf16[1,1,384,128]{3,2,1,0:T(8,128)(2,1)}, u32[]{:S(2)}) copy-start(bf16[1,1,384,128]{3,2,1,0:T(8,128)(2,1)} %g_ref.1) | copy-start | bytes 294916
  4.2 0.7 %copy-start.4 = (s32[4,8,21]{2,1,0:T(8,128)S(1)}, s32[4,8,21]{2,1,0:T(8,128)}, u32[]{:S(2)}) copy-start(s32[4,8,21]{2,1,0:T(8,128)} %list_ref.1) | copy-start | bytes 8068
  4.9 0.7 %copy-start.5 = (s32[4,8]{1,0:T(4,128)S(1)}, s32[4,8]{1,0:T(4,128)}, u32[]{:S(2)}) copy-start(s32[4,8]{1,0:T(4,128)} %count_ref.1) | copy-start | bytes 388

commit v2 on v1

--- a/solution.py
+++ b/solution.py
@@ -26,12 +26,13 @@
 
 def kernel(
     pairs, bands,
-    q_ref, k_ref, v_ref, g_ref, list_ref, count_ref,
-    dq_ref, dk_ref, dv_ref,
+    q_ref, k_ref, v_ref, g_ref, list_hbm, count_hbm,
+    out_ref,
     qbuf, gbuf, kbuf, vbuf, kturn, pstore, gpstore, maxrow, bias, stats, stats_in,
     plow, dslow, dqacc, dkacc, dvacc, dqout, dqin, dkout, dvout, dkin, dvin,
     q_send, q_recv, g_send, g_recv, k_send, k_recv, v_send, v_recv, s_send, s_recv,
     dq_send, dq_recv, dk_send, dk_recv, dv_send, dv_recv,
+    list_ref, count_ref, fetch_sem,
 ):
     rows, width = q_ref.shape[2], q_ref.shape[3]
     scale = width ** -0.5
@@ -49,6 +50,15 @@
     def column(e):
         return 2 * g + p + e * sign
 
+    own = ((q_ref.at[0, 0], qbuf.at[0]), (k_ref.at[0, 0], kbuf.at[0]),
+           (v_ref.at[0, 0], vbuf.at[0]), (g_ref.at[0, 0], gbuf.at[0]),
+           (list_hbm, list_ref), (count_hbm, count_ref))
+    fetches = [
+        pltpu.make_async_copy(src, dst, fetch_sem.at[i]) for i, (src, dst) in enumerate(own)
+    ]
+    for fetch in fetches:
+        fetch.start()
+
     def has_band(place):
         below = jnp.where(place == 1, lat > 0, True)
         above = jnp.where(place == 2, lat < bands - 1, True)
@@ -59,7 +69,7 @@
     barrier = pltpu.get_barrier_semaphore()
     for e in distances:
         pl.semaphore_signal(barrier, inc=1, device_id={"lon": along(e), "lat": lat}, device_id_type=MESH)
-    beside = [(e, place) for e in (0, 1) for place in range(3) if (e, place) != (0, 0)]
+    beside = [(0, 1), (0, 2), (1, 0)]
     for e, place in beside:
         @pl.when(has_band(place))
         def _(e=e, place=place):
@@ -68,11 +78,44 @@
                 device_id={"lon": column(e), "lat": lat + BANDS[place]}, device_id_type=MESH,
             )
 
-    qbuf[0] = q_ref[0, 0]
-    gbuf[0] = g_ref[0, 0]
-    kbuf[0] = k_ref[0, 0]
-    vbuf[0] = v_ref[0, 0]
-
+    n_beside = 1 + jnp.where(lat > 0, 1, 0) + jnp.where(lat < bands - 1, 1, 0)
+    pl.semaphore_wait(barrier, len(distances) + n_beside)
+
+    def remote(src, dst, send, recv, to_lon, to_lat):
+        return pltpu.make_async_remote_copy(
+            src_ref=src, dst_ref=dst, send_sem=send, recv_sem=recv,
+            device_id={"lon": to_lon, "lat": to_lat}, device_id_type=MESH,
+        )
+
+    def key_copies(e, place):
+        here, there = 3 * e + place, 3 * e + BAND_BACK[place]
+        passed = e == 1 and place > 0
+        to = (lon if passed else column(e), lat + BANDS[place])
+        k_src = kbuf.at[3] if passed else k_ref.at[0, 0]
+        v_src = vbuf.at[3] if passed else v_ref.at[0, 0]
+        return (
+            remote(k_src, kbuf.at[there], k_send.at[here], k_recv.at[there], *to),
+            remote(v_src, vbuf.at[there], v_send.at[here], v_recv.at[there], *to),
+        )
+
+    def query_copies(t):
+        to = (along(-PAIR_STEPS[t]), lat)
+        return (
+            remote(q_ref.at[0, 0], qbuf.at[t], q_send.at[t], q_recv.at[t], *to),
+            remote(g_ref.at[0, 0], gbuf.at[t], g_send.at[t], g_recv.at[t], *to),
+        )
+
+    for t in (1, 2, 3):
+        for copy in query_copies(t):
+            copy.start()
+    for e, place in beside:
+        @pl.when(has_band(place))
+        def _(e=e, place=place):
+            for copy in key_copies(e, place):
+                copy.start()
+
+    fetches[4].wait()
+    fetches[5].wait()
     slot = lax.broadcasted_iota(jnp.int32, (8, 1), 0)
     other = jnp.where(slot >= 3, 1, 0)
     place = slot - 3 * other
@@ -91,39 +134,6 @@
 
     stats[0:4] = jnp.full((4, rows), LOWEST, jnp.float32)
     stats[4:16] = jnp.zeros((12, rows), jnp.float32)
-
-    n_beside = 1 + 2 * (jnp.where(lat > 0, 1, 0) + jnp.where(lat < bands - 1, 1, 0))
-    pl.semaphore_wait(barrier, len(distances) + n_beside)
-
-    def remote(src, dst, send, recv, to_lon, to_lat):
-        return pltpu.make_async_remote_copy(
-            src_ref=src, dst_ref=dst, send_sem=send, recv_sem=recv,
-            device_id={"lon": to_lon, "lat": to_lat}, device_id_type=MESH,
-        )
-
-    def key_copies(e, place):
-        here, there = 3 * e + place, 3 * e + BAND_BACK[place]
-        to = (column(e), lat + BANDS[place])
-        return (
-            remote(k_ref.at[0, 0], kbuf.at[there], k_send.at[here], k_recv.at[there], *to),
-            remote(v_ref.at[0, 0], vbuf.at[there], v_send.at[here], v_recv.at[there], *to),
-        )
-
-    def query_copies(t):
-        to = (along(-PAIR_STEPS[t]), lat)
-        return (
-            remote(q_ref.at[0, 0], qbuf.at[t], q_send.at[t], q_recv.at[t], *to),
-            remote(g_ref.at[0, 0], gbuf.at[t], g_send.at[t], g_recv.at[t], *to),
-        )
-
-    for t in (1, 2, 3):
-        for copy in query_copies(t):
-            copy.start()
-    for e, place in beside:
-        @pl.when(has_band(place))
-        def _(e=e, place=place):
-            for copy in key_copies(e, place):
-                copy.start()
 
     dqacc[...] = jnp.zeros_like(dqacc)
     dkacc[...] = jnp.zeros_like(dkacc)
@@ -163,24 +173,48 @@
         stats[4 + t:5 + t] = stats[4 + t:5 + t] * shrink + total
         stats[8 + t:9 + t] = stats[8 + t:9 + t] * shrink + weighted
 
-    for t in range(4):
-        if t > 0:
-            arrived(qbuf, t, q_recv)
-            arrived(gbuf, t, g_recv)
-
-        def first_step(ks, carry, t=t):
+    for fetch in fetches[:4]:
+        fetch.wait()
+
+    def keys_arrive(ks):
+        arrived(kbuf, ks, k_recv)
+        arrived(vbuf, ks, v_recv)
+
+    def turn(ks):
+        kturn[ks] = kbuf[ks].astype(jnp.float32).T.astype(jnp.bfloat16)
+
+    def first_pairs(t, start, stop, fresh=False):
+        def step(ks, carry):
             @pl.when(has_band(ks % 3))
             def _():
-                if t == 0:
-                    @pl.when(ks > 0)
-                    def _():
-                        arrived(kbuf, ks, k_recv)
-                        arrived(vbuf, ks, v_recv)
-                    kturn[ks] = kbuf[ks].astype(jnp.float32).T.astype(jnp.bfloat16)
+                if fresh:
+                    keys_arrive(ks)
+                    turn(ks)
                 first_pair(t, ks)
             return carry
 
-        lax.fori_loop(first_slot(t), 6, first_step, 0)
+        lax.fori_loop(start, stop, step, 0)
+
+    turn(0)
+    first_pair(0, 0)
+    first_pairs(0, 1, 3, fresh=True)
+    keys_arrive(3)
+    for place in (1, 2):
+        @pl.when(has_band(place))
+        def _(place=place):
+            for copy in key_copies(1, place):
+                copy.start()
+    turn(3)
+    first_pair(0, 3)
+    arrived(qbuf, 1, q_recv)
+    arrived(gbuf, 1, g_recv)
+    first_pairs(1, 0, 4)
+    first_pairs(0, 4, 6, fresh=True)
+    first_pairs(1, 4, 6)
+    for t in (2, 3):
+        arrived(qbuf, t, q_recv)
+        arrived(gbuf, t, g_recv)
+        first_pairs(t, first_slot(t), 6)
 
     def stat_copy(i, e):
         back = distances.index(-e % pairs)
@@ -223,60 +257,78 @@
             dqout.at[t], dqin.at[t], dq_send.at[t], dq_recv.at[t], along(PAIR_STEPS[t]), lat
         )
 
-    for t in (3, 1, 2):
-        def second_step(ks, carry, t=t):
+    def send_query_grad(t):
+        dqout[t] = (dqacc[t] * scale).astype(jnp.bfloat16)
+        query_grad_copy(t).start()
+
+    def key_grad_copies(ks):
+        e, place = ks // 3, ks % 3
+        back = 3 * e + BAND_BACK[place]
+        to = (column(1) if ks == 3 else lon, lat + BANDS[place])
+        return (
+            remote(dkout.at[ks], dkin.at[back], dk_send.at[ks], dk_recv.at[back], *to),
+            remote(dvout.at[ks], dvin.at[back], dv_send.at[ks], dv_recv.at[back], *to),
+        )
+
+    def send_key_grad(ks):
+        dkout[ks] = (dkacc[ks] * scale).astype(jnp.bfloat16)
+        dvout[ks] = dvacc[ks].astype(jnp.bfloat16)
+        for copy in key_grad_copies(ks):
+            copy.start()
+
+    def second_pairs(t, start, stop):
+        def step(ks, carry):
             @pl.when(has_band(ks % 3))
             def _():
                 second_pair(t, ks)
             return carry
 
-        lax.fori_loop(first_slot(t), 6, second_step, 0)
-        dqout[t] = (dqacc[t] * scale).astype(jnp.bfloat16)
-        query_grad_copy(t).start()
-
-    def key_grad_copies(ks):
-        e, place = ks // 3, ks % 3
-        back = 3 * e + jnp.where(place == 0, 0, 3 - place)
-        to = (column(e), lat + jnp.where(place == 0, 0, 2 * place - 3))
-        return (
-            remote(dkout.at[ks], dkin.at[back], dk_send.at[ks], dk_recv.at[back], *to),
-            remote(dvout.at[ks], dvin.at[back], dv_send.at[ks], dv_recv.at[back], *to),
-        )
-
-    def last_step(i, carry):
-        ks = 5 - i
-
-        @pl.when(has_band(ks % 3))
-        def _():
-            second_pair(0, ks)
-
-            @pl.when(ks > 0)
-            def _():
-                dkout[ks] = (dkacc[ks] * scale).astype(jnp.bfloat16)
-                dvout[ks] = dvacc[ks].astype(jnp.bfloat16)
-                for copy in key_grad_copies(ks):
-                    copy.start()
-        return carry
-
-    lax.fori_loop(0, 6, last_step, 0)
+        lax.fori_loop(start, stop, step, 0)
+
+    def add_key_grad(ks, into, factor):
+        arrived(dkin, ks, dk_recv)
+        arrived(dvin, ks, dv_recv)
+        dkacc[into] += dkin[ks].astype(jnp.float32) * factor
+        dvacc[into] += dvin[ks].astype(jnp.float32)
+
+    second_pairs(3, 3, 6)
+    send_query_grad(3)
+    second_pairs(1, 3, 6)
+    second_pairs(2, 3, 6)
+    second_pairs(0, 3, 6)
+    for place in (1, 2):
+        @pl.when(has_band(place))
+        def _(place=place):
+            send_key_grad(3 + place)
+    second_pairs(1, 0, 3)
+    send_query_grad(1)
+    for place in (1, 2):
+        @pl.when(has_band(place))
+        def _(place=place):
+            add_key_grad(3 + place, 3, 1.0 / scale)
+    send_key_grad(3)
+    second_pairs(2, 0, 3)
+    send_query_grad(2)
+    second_pairs(0, 1, 3)
+    for place in (1, 2):
+        @pl.when(has_band(place))
+        def _(place=place):
+            send_key_grad(place)
+    second_pair(0, 0)
 
     total = dqacc[0] * scale
     for t in (3, 1, 2):
         arrived(dqin, t, dq_recv)
         total += dqin[t].astype(jnp.float32)
-    dq_ref[0, 0] = total.T.astype(jnp.bfloat16)
-
-    dkacc[0] = dkacc[0] * scale
-    for e, place in reversed(beside):
-        @pl.when(has_band(place))
-        def _(e=e, place=place):
-            ks = 3 * e + place
-            arrived(dkin, ks, dk_recv)
-            arrived(dvin, ks, dv_recv)
-            dkacc[0] += dkin[ks].astype(jnp.float32)
-            dvacc[0] += dvin[ks].astype(jnp.float32)
-    dk_ref[0, 0] = dkacc[0].astype(jnp.bfloat16)
-    dv_ref[0, 0] = dvacc[0].astype(jnp.bfloat16)
+    out_ref[0] = total.T.astype(jnp.bfloat16)
+
+    add_key_grad(3, 0, 1.0 / scale)
+    for place in (1, 2):
+        @pl.when(has_band(place))
+        def _(place=place):
+            add_key_grad(place, 0, 1.0 / scale)
+    out_ref[1] = (dkacc[0] * scale).astype(jnp.bfloat16)
+    out_ref[2] = dvacc[0].astype(jnp.bfloat16)
 
     for t in (1, 2, 3):
         for copy in query_copies(t):
@@ -284,7 +336,7 @@
         query_grad_copy(t).wait_send()
     for i, e in enumerate(distances):
         stat_copy(i, e).wait_send()
-    for e, place in beside:
+    for e, place in beside + [(1, 1), (1, 2)]:
         @pl.when(has_band(place))
         def _(e=e, place=place):
             for copy in key_copies(e, place) + key_grad_copies(3 * e + place):
@@ -293,16 +345,15 @@
 
 def per_device(pairs, bands, queries, keys, values, cotangent, key_tiles, tile_count):
     rows, width = queries.shape[2], queries.shape[3]
-    shape = jax.ShapeDtypeStruct(queries.shape, jnp.bfloat16)
     low, full = jnp.bfloat16, jnp.float32
     n_stats = len({e % pairs for e in range(-3, 4)} - {0})
     vmem = pl.BlockSpec(memory_space=pltpu.VMEM)
     dma = pltpu.SemaphoreType.DMA
-    return pl.pallas_call(
+    grads = pl.pallas_call(
         functools.partial(kernel, pairs, bands),
-        out_shape=(shape, shape, shape),
-        in_specs=[vmem] * 6,
-        out_specs=(vmem, vmem, vmem),
+        out_shape=jax.ShapeDtypeStruct((3, rows, width), low),
+        in_specs=[pl.BlockSpec(memory_space=pl.ANY)] * 6,
+        out_specs=vmem,
         scratch_shapes=[
             pltpu.VMEM((4, rows, width), low),
             pltpu.VMEM((4, rows, width), low),
@@ -331,11 +382,15 @@
             dma((n_stats,)), dma((n_stats,)),
             dma((4,)), dma((4,)),
             dma((6,)), dma((6,)), dma((6,)), dma((6,)),
+            pltpu.VMEM(key_tiles.shape, jnp.int32),
+            pltpu.VMEM(tile_count.shape, jnp.int32),
+            dma((6,)),
         ],
         compiler_params=pltpu.CompilerParams(
-            collective_id=0, has_side_effects=True, vmem_limit_bytes=48 * 1024 * 1024
+            collective_id=0, has_side_effects=True, vmem_limit_bytes=60 * 1024 * 1024
         ),
     )(queries, keys, values, cotangent, key_tiles, tile_count)
+    return tuple(grads[i].reshape(queries.shape) for i in range(3))
 
 
 def solution(mesh):

time: 55.3 us -> 50.3 us (0.910)
  local copies, waits for them, and re-layouts: 6.88 us -> 1.7 us
    unnamed x15 -> x0, local copies, waits for them, and re-layouts: 6.88 us -> none
    another operation x0 -> x1, local copies, waits for them, and re-layouts: none -> 1.7 us  [per_device(): return tuple((grads[i].reshape(queries.shape) for i in range(3)))]
where the time goes in v2:
time: 50.3 us; the launch traced here: 49.9 us
  Pallas kernels  47.6 us (95%)
  local copies, waits for them, and re-layouts  1.7 us (3%)
  between operations  0.64 us (1%)
    pallas_call x1, Pallas kernels, per_device(): pl.pallas_call(functools.partial(kernel, pairs, bands), out_shape=jax.Sha...  47.6 us
    another operation x1, local copies, waits for them, and re-layouts, per_device(): return tuple((grads[i].reshape(queries.shape) for i in range(3)))  1.7 us

profile of v2, /device:TPU:1, one launch (start us, length us, event | category | flops | bytes accessed | tf_op | source)
XLA Modules:
  0.0 49.9 jit_solution(12276534312669870653)
XLA Ops:
  0.6 47.6 %shard_map.85 = bf16[3,384,128]{2,1,0:T(8,128)(2,1)} custom-call(bf16[1,1,384,128]{3,2,1,0:T(8,128)(2,1)} %q_ref.1, bf16[1,1,384,128]{3,2,1,0:T(8,128)(2,1)} %k_ref.1, bf16[1,1,384,128]{3,2,1,0:T(8,128)(2,1)} %v_ref.1, bf16[1,1,384,128]{3,2,1,0:T(8,128)(2,1)} %g_ref.1, s32[4,8,21]{2,1,0:T(8,128)} %list_hbm.1, s32[4,8]{1,0:T(4,128)} %count_hbm.1), custom_call_target="tpu_custom_call" | custom-call | tf_op jit(solution)/shard_map/pallas_call | solution.py:352
  48.2 1.7 %slice_bitcast_fusion = (bf16[1,1,384,128]{3,2,1,0:T(8,128)(2,1)}, bf16[1,1,384,128]{3,2,1,0:T(8,128)(2,1)}, bf16[1,1,384,128]{3,2,1,0:T(8,128)(2,1)}) fusion(bf16[3,384,128]{2,1,0:T(8,128)(2,1)} %shard_map.85), kind=kLoop, calls=%fused_computation | loop fusion | bytes 589824 | tf_op jit(solution)/shard_map/reshape;squeeze | solution.py:393

commit v3 on v2

--- a/solution.py
+++ b/solution.py
@@ -136,13 +136,11 @@
     stats[4:16] = jnp.zeros((12, rows), jnp.float32)
 
     dqacc[...] = jnp.zeros_like(dqacc)
-    dkacc[...] = jnp.zeros_like(dkacc)
-    dvacc[...] = jnp.zeros_like(dvacc)
 
     def arrived(buf, index, recv):
         pltpu.make_async_copy(buf.at[index], buf.at[index], recv.at[index]).wait()
 
-    chunks = [pl.ds(i, 128) for i in range(0, rows, 128)]
+    chunks = [pl.ds(i, 32) for i in range(0, rows, 32)]
 
     def first_slot(t):
         return 3 if t == 3 else 0
@@ -160,13 +158,16 @@
         new = jnp.maximum(old, top)
         shift = new - offset
         gpstore[index] = dot_rows(vbuf[ks], gbuf[t])
-        total = jnp.zeros((1, rows), jnp.float32)
-        weighted = jnp.zeros((1, rows), jnp.float32)
+        total = jnp.zeros((8, rows), jnp.float32)
+        weighted = jnp.zeros((8, rows), jnp.float32)
         for c in chunks:
             powers = jnp.exp2(pstore[index, c, :] * scale2 - shift)
             pstore[index, c, :] = powers
-            total += jnp.sum(powers, axis=0, keepdims=True)
-            weighted += jnp.sum(powers * gpstore[index, c, :], axis=0, keepdims=True)
+            total += jnp.sum(powers.reshape(-1, 8, rows), axis=0)
+            terms = powers * gpstore[index, c, :]
+            weighted += jnp.sum(terms.reshape(-1, 8, rows), axis=0)
+        total = jnp.sum(total, axis=0, keepdims=True)
+        weighted = jnp.sum(weighted, axis=0, keepdims=True)
         shrink = jnp.exp2(old - new)
         maxrow[pl.ds(index, 1), :] = new
         stats[t:t + 1] = new
@@ -183,21 +184,22 @@
     def turn(ks):
         kturn[ks] = kbuf[ks].astype(jnp.float32).T.astype(jnp.bfloat16)
 
-    def first_pairs(t, start, stop, fresh=False):
+    def first_pairs(ts, start, stop, fresh=False):
         def step(ks, carry):
             @pl.when(has_band(ks % 3))
             def _():
                 if fresh:
                     keys_arrive(ks)
                     turn(ks)
-                first_pair(t, ks)
+                for t in ts:
+                    first_pair(t, ks)
             return carry
 
         lax.fori_loop(start, stop, step, 0)
 
     turn(0)
     first_pair(0, 0)
-    first_pairs(0, 1, 3, fresh=True)
+    first_pairs((0,), 1, 3, fresh=True)
     keys_arrive(3)
     for place in (1, 2):
         @pl.when(has_band(place))
@@ -206,15 +208,12 @@
                 copy.start()
     turn(3)
     first_pair(0, 3)
-    arrived(qbuf, 1, q_recv)
-    arrived(gbuf, 1, g_recv)
-    first_pairs(1, 0, 4)
-    first_pairs(0, 4, 6, fresh=True)
-    first_pairs(1, 4, 6)
-    for t in (2, 3):
-        arrived(qbuf, t, q_recv)
-        arrived(gbuf, t, g_recv)
-        first_pairs(t, first_slot(t), 6)
+    first_pairs((0,), 4, 6, fresh=True)
+    for ts in ((1, 2), (3,)):
+        for t in ts:
+            arrived(qbuf, t, q_recv)
+            arrived(gbuf, t, g_recv)
+        first_pairs(ts, first_slot(ts[0]), 6)
 
     def stat_copy(i, e):
         back = distances.index(-e % pairs)
@@ -240,17 +239,22 @@
         inverse = 1.0 / total
         finals.append((top, inverse, weighted * inverse))
 
-    def second_pair(t, ks):
+    def low_terms(t, ks):
         index = stored(t, ks)
         top, inverse, delta = finals[t]
         factor = jnp.exp2(maxrow[pl.ds(index, 1), :] - top) * inverse
+        columns = slice(t * rows, (t + 1) * rows)
         for c in chunks:
             probs = pstore[index, c, :] * factor
-            plow[c, :] = probs.astype(jnp.bfloat16)
-            dslow[c, :] = (probs * (gpstore[index, c, :] - delta)).astype(jnp.bfloat16)
-        dvacc[ks] += dot(plow[...], gbuf[t])
-        dkacc[ks] += dot(dslow[...], qbuf[t])
-        dqacc[t] += dot(kturn[ks], dslow[...])
+            plow[c, columns] = probs.astype(jnp.bfloat16)
+            dslow[c, columns] = (probs * (gpstore[index, c, :] - delta)).astype(jnp.bfloat16)
+
+    def products(first, count, ks):
+        columns = slice(first * rows, (first + count) * rows)
+        dqacc[:, columns] += dot(kturn[ks], dslow[:, columns])
+        value_part = dot(plow[:, columns], gbuf[first:first + count].reshape(-1, width))
+        key_part = dot(dslow[:, columns], qbuf[first:first + count].reshape(-1, width))
+        return key_part, value_part
 
     def query_grad_copy(t):
         return remote(
@@ -258,13 +262,13 @@
         )
 
     def send_query_grad(t):
-        dqout[t] = (dqacc[t] * scale).astype(jnp.bfloat16)
+        dqout[t] = (dqacc[:, t * rows:(t + 1) * rows] * scale).astype(jnp.bfloat16)
         query_grad_copy(t).start()
 
     def key_grad_copies(ks):
         e, place = ks // 3, ks % 3
-        back = 3 * e + BAND_BACK[place]
-        to = (column(1) if ks == 3 else lon, lat + BANDS[place])
+        back = 3 * e + jnp.where(place == 0, 0, 3 - place)
+        to = (jnp.where(ks == 3, column(1), lon), lat + jnp.where(place == 0, 0, 2 * place - 3))
         return (
             remote(dkout.at[ks], dkin.at[back], dk_send.at[ks], dk_recv.at[back], *to),
             remote(dvout.at[ks], dvin.at[back], dv_send.at[ks], dv_recv.at[back], *to),
@@ -276,47 +280,73 @@
         for copy in key_grad_copies(ks):
             copy.start()
 
-    def second_pairs(t, start, stop):
-        def step(ks, carry):
-            @pl.when(has_band(ks % 3))
-            def _():
-                second_pair(t, ks)
-            return carry
-
-        lax.fori_loop(start, stop, step, 0)
-
     def add_key_grad(ks, into, factor):
         arrived(dkin, ks, dk_recv)
         arrived(dvin, ks, dv_recv)
         dkacc[into] += dkin[ks].astype(jnp.float32) * factor
         dvacc[into] += dvin[ks].astype(jnp.float32)
 
-    second_pairs(3, 3, 6)
+    def other_parity(i, carry):
+        place = (i + 1) % 3
+        ks = 3 + place
+
+        @pl.when(has_band(place))
+        def _():
+            for t in (3, 2, 1, 0):
+                low_terms(t, ks)
+            key_late, value_late = products(2, 2, ks)
+            key_early, value_early = products(0, 2, ks)
+            dkacc[ks] = key_late + key_early
+            dvacc[ks] = value_late + value_early
+
+            @pl.when(place > 0)
+            def _():
+                send_key_grad(ks)
+        return carry
+
+    lax.fori_loop(0, 3, other_parity, 0)
     send_query_grad(3)
-    second_pairs(1, 3, 6)
-    second_pairs(2, 3, 6)
-    second_pairs(0, 3, 6)
-    for place in (1, 2):
-        @pl.when(has_band(place))
-        def _(place=place):
-            send_key_grad(3 + place)
-    second_pairs(1, 0, 3)
-    send_query_grad(1)
+
+    def neighbours(ks):
+        for t in (1, 2):
+            low_terms(t, ks)
+        dkacc[ks], dvacc[ks] = products(1, 2, ks)
+
+    neighbours(0)
     for place in (1, 2):
         @pl.when(has_band(place))
         def _(place=place):
             add_key_grad(3 + place, 3, 1.0 / scale)
     send_key_grad(3)
-    second_pairs(2, 0, 3)
+
+    def same_parity(ks, carry):
+        @pl.when(has_band(ks))
+        def _():
+            neighbours(ks)
+        return carry
+
+    lax.fori_loop(1, 3, same_parity, 0)
+    send_query_grad(1)
     send_query_grad(2)
-    second_pairs(0, 1, 3)
-    for place in (1, 2):
-        @pl.when(has_band(place))
-        def _(place=place):
-            send_key_grad(place)
-    second_pair(0, 0)
-
-    total = dqacc[0] * scale
+
+    def own_queries(i, carry):
+        ks = (i + 1) % 3
+
+        @pl.when(has_band(ks))
+        def _():
+            low_terms(0, ks)
+            key_part, value_part = products(0, 1, ks)
+            dkacc[ks] += key_part
+            dvacc[ks] += value_part
+
+            @pl.when(ks > 0)
+            def _():
+                send_key_grad(ks)
+        return carry
+
+    lax.fori_loop(0, 3, own_queries, 0)
+
+    total = dqacc[:, :rows] * scale
     for t in (3, 1, 2):
         arrived(dqin, t, dq_recv)
         total += dqin[t].astype(jnp.float32)
@@ -366,9 +396,9 @@
             pltpu.VMEM((4, 8, rows), full),
             pltpu.VMEM((16, rows), full),
             pltpu.VMEM((n_stats, 16, rows), full),
-            pltpu.VMEM((rows, rows), low),
-            pltpu.VMEM((rows, rows), low),
-            pltpu.VMEM((4, width, rows), full),
+            pltpu.VMEM((rows, 4 * rows), low),
+            pltpu.VMEM((rows, 4 * rows), low),
+            pltpu.VMEM((width, 4 * rows), full),
             pltpu.VMEM((6, rows, width), full),
             pltpu.VMEM((6, rows, width), full),
             pltpu.VMEM((4, width, rows), low),

time: 50.3 us -> 44.8 us (0.89)
  Pallas kernels: 47.6 us -> 42.3 us
    pallas_call x1, Pallas kernels: 47.6 us -> 42.3 us  [per_device(): pl.pallas_call(functools.partial(kernel, pairs, bands), out_shape=jax.Sha...]
where the time goes in v3:
time: 44.8 us; the launch traced here: 44.6 us
  Pallas kernels  42.3 us (94%)
  local copies, waits for them, and re-layouts  1.7 us (4%)
  between operations  0.64 us (1%)
    pallas_call x1, Pallas kernels, per_device(): pl.pallas_call(functools.partial(kernel, pairs, bands), out_shape=jax.Sha...  42.3 us
    another operation x1, local copies, waits for them, and re-layouts, per_device(): return tuple((grads[i].reshape(queries.shape) for i in range(3)))  1.7 us

profile of v3, /device:TPU:1, one launch (start us, length us, event | category | flops | bytes accessed | tf_op | source)
XLA Modules:
  0.0 44.6 jit_solution(9960400491335765027)
XLA Ops:
  0.6 42.3 %shard_map.85 = bf16[3,384,128]{2,1,0:T(8,128)(2,1)} custom-call(bf16[1,1,384,128]{3,2,1,0:T(8,128)(2,1)} %q_ref.1, bf16[1,1,384,128]{3,2,1,0:T(8,128)(2,1)} %k_ref.1, bf16[1,1,384,128]{3,2,1,0:T(8,128)(2,1)} %v_ref.1, bf16[1,1,384,128]{3,2,1,0:T(8,128)(2,1)} %g_ref.1, s32[4,8,21]{2,1,0:T(8,128)} %list_hbm.1, s32[4,8]{1,0:T(4,128)} %count_hbm.1), custom_call_target="tpu_custom_call" | custom-call | tf_op jit(solution)/shard_map/pallas_call | solution.py:382
  42.9 1.7 %slice_bitcast_fusion = (bf16[1,1,384,128]{3,2,1,0:T(8,128)(2,1)}, bf16[1,1,384,128]{3,2,1,0:T(8,128)(2,1)}, bf16[1,1,384,128]{3,2,1,0:T(8,128)(2,1)}) fusion(bf16[3,384,128]{2,1,0:T(8,128)(2,1)} %shard_map.85), kind=kLoop, calls=%fused_computation | loop fusion | bytes 589824 | tf_op jit(solution)/shard_map/reshape;squeeze | solution.py:423

commit v4 on v3

--- a/solution.py
+++ b/solution.py
@@ -98,6 +98,17 @@
             remote(v_src, vbuf.at[there], v_send.at[here], v_recv.at[there], *to),
         )
 
+    line = pairs == 4
+    inner = jnp.logical_and(g > 0, g < 3)
+    inner_slot = jnp.where((g == 1) == (p == 0), 1, 2)
+
+    def hand_on():
+        to = (jnp.where(g == 1, lon - 2, lon + 2), lat)
+        return (
+            remote(qbuf.at[inner_slot], qbuf.at[3], q_send.at[3], q_recv.at[3], *to),
+            remote(gbuf.at[inner_slot], gbuf.at[3], g_send.at[3], g_recv.at[3], *to),
+        )
+
     def query_copies(t):
         to = (along(-PAIR_STEPS[t]), lat)
         return (
@@ -105,9 +116,15 @@
             remote(g_ref.at[0, 0], gbuf.at[t], g_send.at[t], g_recv.at[t], *to),
         )
 
-    for t in (1, 2, 3):
+    for t in (1, 2):
         for copy in query_copies(t):
             copy.start()
+
+    @pl.when(jnp.logical_not(inner) if line else True)
+    def _():
+        for copy in query_copies(3):
+            copy.start()
+
     for e, place in beside:
         @pl.when(has_band(place))
         def _(e=e, place=place):
@@ -206,13 +223,25 @@
         def _(place=place):
             for copy in key_copies(1, place):
                 copy.start()
+    if line:
+        @pl.when(inner)
+        def _():
+            arrived(qbuf, inner_slot, q_recv)
+            arrived(gbuf, inner_slot, g_recv)
+            for copy in hand_on():
+                copy.start()
+
     turn(3)
     first_pair(0, 3)
     first_pairs((0,), 4, 6, fresh=True)
     for ts in ((1, 2), (3,)):
         for t in ts:
-            arrived(qbuf, t, q_recv)
-            arrived(gbuf, t, g_recv)
+            taken = jnp.logical_and(inner, inner_slot == t)
+
+            @pl.when(jnp.logical_not(taken) if line else True)
+            def _(t=t):
+                arrived(qbuf, t, q_recv)
+                arrived(gbuf, t, g_recv)
         first_pairs(ts, first_slot(ts[0]), 6)
 
     def stat_copy(i, e):

time: 44.8 us -> 41.8 us (0.933)
  Pallas kernels: 42.3 us -> 39.4 us
    pallas_call x1, Pallas kernels: 42.3 us -> 39.4 us  [per_device(): pl.pallas_call(functools.partial(kernel, pairs, bands), out_shape=jax.Sha...]
where the time goes in v4:
time: 41.8 us; the launch traced here: 41.7 us
  Pallas kernels  39.4 us (94%)
  local copies, waits for them, and re-layouts  1.7 us (4%)
  between operations  0.64 us (2%)
    pallas_call x1, Pallas kernels, per_device(): pl.pallas_call(functools.partial(kernel, pairs, bands), out_shape=jax.Sha...  39.4 us
    another operation x1, local copies, waits for them, and re-layouts, per_device(): return tuple((grads[i].reshape(queries.shape) for i in range(3)))  1.7 us

profile of v4, /device:TPU:1, one launch (start us, length us, event | category | flops | bytes accessed | tf_op | source)
XLA Modules:
  0.0 41.7 jit_solution(14589625556967034063)
XLA Ops:
  0.6 39.4 %shard_map.85 = bf16[3,384,128]{2,1,0:T(8,128)(2,1)} custom-call(bf16[1,1,384,128]{3,2,1,0:T(8,128)(2,1)} %q_ref.1, bf16[1,1,384,128]{3,2,1,0:T(8,128)(2,1)} %k_ref.1, bf16[1,1,384,128]{3,2,1,0:T(8,128)(2,1)} %v_ref.1, bf16[1,1,384,128]{3,2,1,0:T(8,128)(2,1)} %g_ref.1, s32[4,8,21]{2,1,0:T(8,128)} %list_hbm.1, s32[4,8]{1,0:T(4,128)} %count_hbm.1), custom_call_target="tpu_custom_call" | custom-call | tf_op jit(solution)/shard_map/pallas_call | solution.py:411
  40.0 1.7 %slice_bitcast_fusion = (bf16[1,1,384,128]{3,2,1,0:T(8,128)(2,1)}, bf16[1,1,384,128]{3,2,1,0:T(8,128)(2,1)}, bf16[1,1,384,128]{3,2,1,0:T(8,128)(2,1)}) fusion(bf16[3,384,128]{2,1,0:T(8,128)(2,1)} %shard_map.85), kind=kLoop, calls=%fused_computation | loop fusion | bytes 589824 | tf_op jit(solution)/shard_map/reshape;squeeze | solution.py:452
